TPU v7x, 32 devices: a whole 2x2x4 slice. The times are simulated.
32 devices in a mesh: fold: 8 (over z, x), blk: 4 (over y, core).
Axes of the slice: x: 2, y: 2, z: 4, core: 2. Of those that a mesh axis runs over, the one named last changes fastest.
Arguments:
- genotypes: bfloat16 [65536, 4096], P('fold', 'blk'), may hold values from 0 to 2, as said below
- phenotypes: bfloat16 [32, 65536], P(None, 'fold'), may hold values from -4 to 4
- trait_order: int32 [32], replicated, may hold values from 0 to 31, each once
Outputs:
- predict: float32 [32, 65536], P('blk', 'fold')
Inputs may be any that keep to these rules, and one draw needn't show every extreme that they name: `genotypes`: dosages are 0, 1 or 2. `trait_order`: a permutation of the 32 traits.
All inputs are finite; a program needn't handle non-finite values.
Results may differ from a plain program's by a relative error of at most 0.00235.
Values may be sent and summed in bfloat16 or wider, within the bound.
A program may use at most 320 MiB of HBM per device.

v0:
```python
import jax
import jax.numpy as jnp
from jax import lax
from jax.sharding import PartitionSpec as P

B = 512
ITERS = 8


LAMBDAS = (0.2, 2.0)
LEVEL_ONE = 0.1
EPSILON = 1e-06


def chebyshev(times_system, target, low_edge, high_edge):
    center = 0.5 * (high_edge + low_edge)
    radius = 0.5 * (high_edge - low_edge)
    sigma_ratio = center / radius
    rho_now = 1.0 / sigma_ratio
    direction = target / center
    solution = jnp.zeros_like(target)
    residual = target
    for iteration in range(ITERS):
        solution = solution + direction
        if iteration + 1 < ITERS:
            residual = residual - times_system(direction)
            rho_next = 1.0 / (2.0 * sigma_ratio - rho_now)
            direction = rho_next * rho_now * direction + 2.0 * rho_next / radius * residual
            rho_now = rho_next
    return solution


def local_gram(geno_blocks):
    return jnp.einsum("sbi,sbj->bij", geno_blocks, geno_blocks, preferred_element_type=jnp.float32)


def per_device(genotypes, phenotypes, trait_order):
    n_fold = lax.axis_size("fold")
    sample_rows = genotypes.shape[0]
    block_count = genotypes.shape[1] // B
    total_rows = sample_rows * n_fold
    held_rows = float(total_rows - sample_rows)
    geno_blocks = genotypes.reshape(sample_rows, block_count, B)
    phen = jnp.take(phenotypes, trait_order, axis=0)
    unit_row = jnp.ones((1, sample_rows), jnp.bfloat16)
    col_local = jnp.dot(unit_row, genotypes, preferred_element_type=jnp.float32).reshape(
        block_count, B
    )
    phen_local = jnp.sum(phen.astype(jnp.float32), axis=1)
    cross_local = jnp.einsum("ps,sbi->bpi", phen, geno_blocks, preferred_element_type=jnp.float32)
    col_total, phen_total = lax.psum((col_local, phen_local), "fold")
    gram_part = local_gram(geno_blocks)
    gram_sum, cross_total = lax.psum((gram_part, cross_local), "fold")
    mean_dose = col_total / total_rows
    inv_scale = 1.0 / jnp.sqrt(
        jnp.diagonal(gram_sum, axis1=1, axis2=2) / total_rows - mean_dose * mean_dose + EPSILON
    )
    gram_out = gram_sum - gram_part
    col_out = col_total - col_local
    cross_out = cross_total - cross_local
    phen_out = phen_total - phen_local
    centered = (
        gram_out
        - col_out[:, :, None] * mean_dose[:, None, :]
        - mean_dose[:, :, None] * col_out[:, None, :]
        + held_rows * mean_dose[:, :, None] * mean_dose[:, None, :]
    )
    system = inv_scale[:, :, None] * centered * inv_scale[:, None, :] / held_rows
    target = (
        (cross_out - phen_out[None, :, None] * mean_dose[:, None, :])
        * inv_scale[:, None, :]
        / held_rows
    )
    bound = jnp.max(jnp.sum(jnp.abs(system), axis=2), axis=1)
    penalty = jnp.array(LAMBDAS, jnp.float32)
    low_edge = jnp.broadcast_to(penalty[None, :, None, None], (block_count, penalty.shape[0], 1, 1))
    high_edge = low_edge + bound[:, None, None, None]

    def times_system(direction):
        return (
            jnp.einsum(
                "brpi,bij->brpj",
                direction,
                system,
                precision=lax.Precision.HIGHEST,
                preferred_element_type=jnp.float32,
            )
            + low_edge * direction
        )

    stacked = jnp.broadcast_to(target[:, None], (block_count, penalty.shape[0]) + target.shape[1:])
    coef = chebyshev(times_system, stacked, low_edge, high_edge)
    scaled = (inv_scale[:, None, None, :] * coef).astype(jnp.bfloat16)
    product = jnp.einsum("sbi,brpi->pbrs", geno_blocks, scaled, preferred_element_type=jnp.float32)
    offset = jnp.einsum(
        "bi,brpi->pbr", mean_dose, scaled.astype(jnp.float32), precision=lax.Precision.HIGHEST
    )
    feature = (product - offset[:, :, :, None]).astype(jnp.bfloat16)
    owned = lax.all_to_all(feature, "blk", split_axis=0, concat_axis=1, tiled=True)
    own_traits = owned.shape[0]
    feature_count = owned.shape[1] * owned.shape[2]
    level_feat = owned.reshape(own_traits, feature_count, sample_rows)
    target_own = lax.dynamic_slice_in_dim(phen, lax.axis_index("blk") * own_traits, own_traits, 0)
    hgram_own = jnp.einsum(
        "pqs,pts->pqt", level_feat, level_feat, preferred_element_type=jnp.float32
    )
    hcross_own = jnp.einsum(
        "pqs,ps->pq", level_feat, target_own, preferred_element_type=jnp.float32
    )
    hgram_total, hcross_total = lax.psum((hgram_own, hcross_own), "fold")
    hgram_out = hgram_total - hgram_own
    hcross_out = hcross_total - hcross_own
    trace_sum = jnp.trace(hgram_out, axis1=1, axis2=2)
    level_system = hgram_out / held_rows + (LEVEL_ONE * trace_sum / (held_rows * feature_count))[
        :, None, None
    ] * jnp.eye(feature_count, dtype=jnp.float32)
    factor = jnp.linalg.cholesky(level_system)
    weight = jax.scipy.linalg.cho_solve((factor, True), (hcross_out / held_rows)[:, :, None])[
        :, :, 0
    ]
    return jnp.einsum(
        "pq,pqs->ps", weight, level_feat.astype(jnp.float32), precision=lax.Precision.HIGHEST
    )


def solution(mesh):
    return jax.shard_map(
        per_device,
        mesh=mesh,
        in_specs=(P("fold", "blk"), P(None, "fold"), P()),
        out_specs=P("blk", "fold"),
        check_vma=False,
    )
```

profile of v0, /device:TPU:0, one launch (start us, length us, event | category | flops | bytes accessed | tf_op | source)
XLA Modules:
  0.0 350.2 jit_solution(9825379027724208222)
XLA Ops:
  6.5 0.7 compare_select_fusion
  7.3 0.7 compare_and_fusion
  7.9 18.2 %fusion.4 = f32[2,512,512]{1,2,0:T(8,128)} fusion(bf16[1024,2,8,512]{3,2,1,0:T(8,128)(2,1)} %bitcast.153), kind=kOutput, calls=%fused_computation.6 | convolution fusion | flops 8589934592 | bytes 18874368 | tf_op jit(solution)/shard_map/sbi,sbj->bij/dot_general | solution.py:34
  26.1 0.9 gather_fusion.1
  27.3 8.0 %fusion.91 = f32[2,32,512]{2,1,0:T(8,128)} fusion(bf16[1024,2,8,512]{3,2,1,0:T(8,128)(2,1)} %bitcast.154, bf16[32,8192]{1,0:T(8,128)(2,1)S(1)} %get-tuple-element.14), kind=kOutput, calls=%fused_computation.52 | convolution fusion | flops 536870912 | bytes 17432576 | tf_op jit(solution)/shard_map/ps,sbi->bpi/dot_general | solution.py:50
  35.3 27.9 %reshape.748 = bf16[8192,2,512]{2,1,0:T(2,128)(2,1)} reshape(bf16[8192,1024]{1,0:T(8,128)(2,1)} %param.4) | data formatting | bytes 33554432 | tf_op jit(solution)/shard_map/reshape | solution.py:43
  63.2 7.1 %fusion = f32[1,2,512]{2,0,1:T(1,128)S(1)} fusion(bf16[1024,2,8,512]{3,2,1,0:T(8,128)(2,1)} %bitcast.155), kind=kOutput, calls=%fused_computation.2 | convolution fusion | flops 16777216 | bytes 16781312 | tf_op jit(solution)/shard_map/dot_general | solution.py:46
  70.3 23.5 %all-reduce.1 = (f32[2,512]{1,0:T(2,128)S(1)}, f32[32]{0:T(128)S(1)}) all-reduce(f32[2,512]{1,0:T(2,128)S(1)} %bitcast.163, f32[32]{0:T(128)S(1)} %get-tuple-element.13), channel_id=1, replica_groups=mesh['fold'=8,'blk'=4] {'fold'}, use_global_device_ids=true, to_apply=%region_1.2 | all-reduce | flops 1056 | bytes 8448 | tf_op jit(solution)/shard_map/psum | solution.py:51
  93.9 51.2 %all-reduce.5.cloned.1.call-done = (f32[2,512,512]{1,2,0:T(8,128)}, f32[2,32,512]{2,1,0:T(8,128)}) async-done(((f32[2,512,512]{1,2,0:T(8,128)}, f32[2,32,512]{2,1,0:T(8,128)}), (f32[2,512,512]{1,2,0:T(8,128)}, f32[2,32,512]{2,1,0:T(8,128)})) %all-reduce.5.cloned.1.call-update) | async-done | bytes 2228240 | tf_op jit(solution)/shard_map/psum | solution.py:53
  145.0 60.1 %copy.105 = f32[2,512,512]{0,2,1:T(8,128)} copy(f32[2,512,512]{1,2,0:T(8,128)} %get-tuple-element.9) | data formatting | bytes 4194304 | tf_op jit(solution)/shard_map/psum | solution.py:53
  205.2 5.5 %gather_fusion = f32[512,2]{1,0:T(8,128)S(1)} fusion(f32[2,512,512]{0,2,1:T(8,128)} %copy.105, s32[512]{0:T(512)S(1)} %bitcast.156), kind=kCustom, calls=%fused_computation | custom fusion | bytes 12288 | tf_op jit(solution)/shard_map/jit(diagonal)/gather | solution.py:56
  210.9 3.0 abs_reduce_fusion
  214.3 2.2 fusion.37
  216.5 2.2 fusion.43
  218.7 2.2 multiply_add_fusion.2
  220.9 2.1 fusion.55
  223.0 2.2 fusion.61
  225.2 2.2 fusion.67
  227.4 2.2 fusion.88
  229.9 12.4 %fusion.17 = bf16[32,2,2,8192]{3,0,2,1:T(8,128)(2,1)S(1)} fusion(bf16[2,2,32,512]{3,2,1,0:T(8,128)(2,1)S(1)} %fusion.88, bf16[8192,2,512,1]{2,1,0,3:T(2,128)(2,1)} %bitcast.157, f32[32,2,2]{0,2,1:T(2,128)S(1)} %bitcast.164), kind=kOutput, calls=%fused_computation.15 | convolution fusion | flops 1075838976 | bytes 19005952 | tf_op jit(solution)/shard_map/sbi,brpi->pbrs/dot_general | solution.py:94
  242.3 3.5 %copy.116 = bf16[32,2,2,8192]{3,2,1,0:T(2,128)(2,1)} copy(bf16[32,2,2,8192]{3,0,2,1:T(8,128)(2,1)S(1)} %fusion.17) | data formatting | bytes 4194304 | tf_op jit(solution)/shard_map/convert_element_type | solution.py:98
  245.9 3.6 %all-to-all-start = ((bf16[32,2,2,8192]{3,2,1,0:T(2,128)(2,1)}), bf16[32,2,2,8192]{3,2,1,0:T(2,128)(2,1)S(1)}, u32[]{:S(2)}, u32[]{:S(2)}) async-start(bf16[32,2,2,8192]{3,2,1,0:T(2,128)(2,1)} %copy.116), calls=%async_computation | async-start | bytes 4194304 | tf_op jit(solution)/shard_map/all_to_all | solution.py:99
  249.5 25.6 %all-to-all-done = bf16[32,2,2,8192]{3,2,1,0:T(2,128)(2,1)S(1)} async-done(((bf16[32,2,2,8192]{3,2,1,0:T(2,128)(2,1)}), bf16[32,2,2,8192]{3,2,1,0:T(2,128)(2,1)S(1)}, u32[]{:S(2)}, u32[]{:S(2)}) %all-to-all-start) | async-done | bytes 2097184 | tf_op jit(solution)/shard_map/all_to_all | solution.py:99
  275.1 3.2 copy.189
  278.3 2.7 reshape.749
  281.1 1.0 fusion.135
  282.0 0.9 fusion.95
  282.9 35.9 %all-reduce = (f32[8,16]{1,0:T(8,128)S(1)}, f32[8,16,16]{2,1,0:T(8,128)S(1)}) all-reduce(f32[8,16]{1,0:T(8,128)S(1)} %bitcast.160, f32[8,16,16]{2,1,0:T(8,128)S(1)} %fusion.135), channel_id=1, replica_groups=mesh['fold'=8,'blk'=4] {'fold'}, use_global_device_ids=true, to_apply=%region_11.12 | all-reduce | flops 2176 | bytes 17408 | tf_op jit(solution)/shard_map/psum | solution.py:110
  319.1 11.7 %custom-call.11 = f32[8,16,16]{2,1,0:T(8,128)S(1)} custom-call(f32[8,16,16]{2,1,0:T(8,128)S(1)} %fusion.115), custom_call_target="Cholesky" | custom-call | tf_op jit(solution)/shard_map/jit(cholesky)/cholesky | solution.py:117
  331.1 9.8 %custom-call.12 = f32[8,1,16,16]{2,3,1,0:T(8,128)S(1)} custom-call(f32[8,1,16,16]{3,2,1,0:T(8,128)S(1)} %select_bitcast_fusion), custom_call_target="InvertDiagBlocksLowerTriangular" | custom-call | tf_op jit(solution)/shard_map/jit(_cho_solve)/vmap()/triangular_solve | solution.py:118
  341.5 1.0 fusion.136
  342.5 0.9 copy.190
  (39 shorter events, 2.3 us)
Async XLA Ops:
  6.5 19.6 %copy-start = (bf16[32,8192]{1,0:T(8,128)(2,1)S(1)}, bf16[32,8192]{1,0:T(8,128)(2,1)}, u32[]{:S(2)}) copy-start(bf16[32,8192]{1,0:T(8,128)(2,1)} %param.5) | copy-start | bytes 1572868
  6.5 138.5 %all-reduce.5.cloned.1.call-start = ((), (), s32[]{:S(2)}) async-start(), calls=%async_computation.1 | async-start | bytes 4456448 | tf_op jit(solution)/shard_map/psum | solution.py:53
  210.9 3.2 copy-start.1
  210.9 3.2 copy-start.2
  210.9 3.3 copy-start.3
  210.9 3.3 copy-start.4
  245.9 29.3 %all-to-all-start = ((bf16[32,2,2,8192]{3,2,1,0:T(2,128)(2,1)}), bf16[32,2,2,8192]{3,2,1,0:T(2,128)(2,1)S(1)}, u32[]{:S(2)}, u32[]{:S(2)}) async-start(bf16[32,2,2,8192]{3,2,1,0:T(2,128)(2,1)} %copy.116), calls=%async_computation | async-start | bytes 4194304 | tf_op jit(solution)/shard_map/all_to_all | solution.py:99
Sparse Core Ops, SparseCore 0:
  35.5 109.5 all-reduce.4
where the time goes:
time: 352 us; the launch traced here: 350 us
  local copies, waits for them, and re-layouts  105 us (30%)
  waiting for transfers between devices  76.8 us (22%)
  matrix products  64.6 us (18%)
  blocking collectives  59.4 us (17%)
  other arithmetic  27.2 us (8%)
  between operations  13.7 us (4%)
  starting transfers between devices  3.61 us (1%)
    psum x1, local copies, waits for them, and re-layouts, per_device(): gram_sum, cross_total = lax.psum((gram_part, cross_local), 'fold')  60.1 us
    psum x1, waiting for transfers between devices, per_device(): gram_sum, cross_total = lax.psum((gram_part, cross_local), 'fold')  51.2 us
    psum x1, blocking collectives, per_device(): hgram_total, hcross_total = lax.psum((hgram_own, hcross_own), 'fold')  35.9 us
    reshape x1, local copies, waits for them, and re-layouts, per_device(): geno_blocks = genotypes.reshape(sample_rows, block_count, B)  27.9 us
    all_to_all x1, waiting for transfers between devices, per_device(): lax.all_to_all(feature, 'blk', split_axis=0, concat_axis=1, tiled=True)  25.6 us
    psum x1, blocking collectives, per_device(): col_total, phen_total = lax.psum((col_local, phen_local), 'fold')  23.5 us
    dot_general x1, matrix products, local_gram(): jnp.einsum('sbi,sbj->bij', geno_blocks, geno_blocks, preferred_element_ty...  18.2 us
    dot_general x7, matrix products, times_system(): jnp.einsum('brpi,bij->brpj', direction, system, precision=lax.Precision.H...  15.3 us
  transfers between devices with their start and end apart: 2, of which 2 were waited for; matrix products, arithmetic and copies ran while one was open for 10% of the time, Pallas kernels for 0%

commit v1 on v0

v1 whole, which is shorter than its diff:
```python
import functools

import jax
import jax.numpy as jnp
from jax import lax
from jax.experimental import pallas as pl
from jax.experimental.pallas import tpu as pltpu
from jax.sharding import PartitionSpec as P

B = 512
T = 128
ITERS = 8
LAMBDAS = (0.2, 2.0)
R = len(LAMBDAS)
LEVEL_ONE = 0.1
EPSILON = 1e-06
CHUNK = 1024
TILES = [(i, j) for i in range(B // T) for j in range(i, B // T)]
PACK = len(TILES) * T
HIGH = lax.Precision.HIGHEST
F32 = jnp.float32
BF16 = jnp.bfloat16
MESH = pl.DeviceIdType.MESH


def dot_nt(a, b):
    return lax.dot_general(a, b, (((1,), (1,)), ((), ())), preferred_element_type=F32)


def dot_nn(a, b, precision=None):
    return lax.dot_general(
        a, b, (((1,), (0,)), ((), ())), preferred_element_type=F32, precision=precision
    )


def iota(shape, axis):
    return lax.broadcasted_iota(jnp.int32, shape, axis)


def down(row):
    return jnp.transpose(jnp.broadcast_to(row, (T, row.shape[1])))


def kernel(
    n_f, n_b, order_ref, phen_ref, geno_ref, out_ref,
    xbuf, pa, gram, cross, gsend, grecv, gfull, csend, crecv, cfull, stats,
    s_hi, s_lo, fsend, frecv, hbuf,
    x_sem, gs_sem, gr_sem, cs_sem, cr_sem, ss_sem, sr_sem,
    g2s_sem, g2r_sem, c2s_sem, c2r_sem, fs_sem, fr_sem, fl_sem, hs_sem, hr_sem,
):
    rows = geno_ref.shape[0]
    blocks = geno_ref.shape[1] // B
    traits = phen_ref.shape[0]
    own = traits // n_b
    group = R * own
    q_total = n_b * blocks * R
    lanes = q_total * own
    g_rows = PACK // n_f
    c_rows = (B // T) * traits // n_f
    chunks = rows // CHUNK
    total_rows = float(rows * n_f)
    held = float(rows * (n_f - 1))
    me_f = lax.axis_index("fold")
    me_b = lax.axis_index("blk")

    def load(b, c):
        part = pl.ds(c * CHUNK, CHUNK)
        return pltpu.make_async_copy(
            geno_ref.at[part, pl.ds(b * B, B)], xbuf.at[b, part], x_sem.at[b, c]
        )

    for b in range(blocks):
        for c in range(chunks):
            load(b, c).start()

    fold_peers = [lax.rem(me_f + off, n_f) for off in range(1, n_f)]
    blk_peers = [lax.rem(me_b + off, n_b) for off in range(1, n_b)]
    barrier = pltpu.get_barrier_semaphore()
    for peer in fold_peers:
        pl.semaphore_signal(barrier, inc=1, device_id=(peer, me_b), device_id_type=MESH)
    for peer in blk_peers:
        pl.semaphore_signal(barrier, inc=1, device_id=(me_f, peer), device_id_type=MESH)

    pick = (iota((traits, traits), 0) == order_ref[...]).astype(F32).T.astype(BF16)
    pa[traits:, :] = jnp.ones((16, rows), BF16)

    @pl.loop(0, chunks)
    def _(c):
        part = pl.ds(pl.multiple_of(c * CHUNK, CHUNK), CHUNK)
        pa[:traits, part] = dot_nn(pick, phen_ref[:, part]).astype(BF16)

    psum_row = dot_nt(pa[traits:, :], pa[:traits, :])[:1, :]

    def fold_copy(src, dst, send, recv, peer):
        return pltpu.make_async_remote_copy(
            src_ref=src, dst_ref=dst, send_sem=send, recv_sem=recv,
            device_id=(peer, me_b), device_id_type=MESH,
        )

    pending = []
    first = [[] for _ in range(blocks)]
    small = [[] for _ in range(blocks)]
    second = [[] for _ in range(blocks)]

    for b in range(blocks):
        gram[...] = jnp.zeros_like(gram)
        cross[...] = jnp.zeros_like(cross)

        @pl.loop(0, chunks)
        def _(c, b=b):
            start = pl.multiple_of(c * CHUNK, CHUNK)
            load(b, c).wait()
            x = xbuf[b, pl.ds(start, CHUNK), :]
            xt = x.T
            half = B // 2
            gram[:half, :] += dot_nn(xt[:half], x)
            gram[half:, half:] += dot_nn(xt[half:], x[:, half:])
            cross[...] += dot_nn(pa[:, pl.ds(start, CHUNK)], x)

        col = cross[traits : traits + 1, :]
        col_down = down(col)
        mean_row = col * (1.0 / rows)
        diag = []
        eye = iota((T, T), 0) == iota((T, T), 1)
        for slot, (i, j) in enumerate(TILES):
            si, sj = slice(i * T, (i + 1) * T), slice(j * T, (j + 1) * T)
            tile = gram[si, sj] - col_down[si, :] * mean_row[:, sj]
            if i == j:
                diag.append(jnp.sum(jnp.where(eye, tile, 0.0), axis=0, keepdims=True))
            gsend[b, slot * T : (slot + 1) * T, :] = tile.astype(BF16)
        psum_down = jnp.transpose(jnp.broadcast_to(psum_row, (T, traits)))
        for i in range(B // T):
            si = slice(i * T, (i + 1) * T)
            csend[b, i * traits : (i + 1) * traits, :] = (
                cross[:traits, si] - psum_down * mean_row[:, si]
            )
        wide_psum = jnp.concatenate([psum_row, jnp.zeros((1, B - traits), F32)], axis=1)
        stats[b, me_f] = jnp.concatenate(
            [col, jnp.concatenate(diag, axis=1), wide_psum, jnp.zeros((5, B), F32)], axis=0
        )
        if b == 0:
            pl.semaphore_wait(barrier, n_f + n_b - 2)
        for k, peer in enumerate(fold_peers):
            sm = fold_copy(
                stats.at[b, me_f], stats.at[b, me_f], ss_sem.at[b, k], sr_sem.at[b, k], peer
            )
            gc = fold_copy(
                gsend.at[b, pl.ds(peer * g_rows, g_rows)], grecv.at[b, me_f],
                gs_sem.at[b, k], gr_sem.at[b, k], peer,
            )
            cc = fold_copy(
                csend.at[b, pl.ds(peer * c_rows, c_rows)], crecv.at[b, me_f],
                cs_sem.at[b, k], cr_sem.at[b, k], peer,
            )
            for copy in (sm, gc, cc):
                copy.start()
            small[b].append(sm)
            first[b] += [gc, cc]
            pending += [sm, gc, cc]

    for b in range(blocks):
        g_mine = pl.ds(me_f * g_rows, g_rows)
        c_mine = pl.ds(me_f * c_rows, c_rows)
        grecv[b, me_f] = gsend[b, g_mine, :]
        crecv[b, me_f] = csend[b, c_mine, :]
        for copy in first[b]:
            copy.wait_recv()
        g_sum = grecv[b, 0].astype(F32)
        c_sum = crecv[b, 0]
        for j in range(1, n_f):
            g_sum += grecv[b, j].astype(F32)
            c_sum += crecv[b, j]
        gfull[b, g_mine, :] = g_sum.astype(BF16)
        cfull[b, c_mine, :] = c_sum
        for k, peer in enumerate(fold_peers):
            gc = fold_copy(
                gfull.at[b, g_mine], gfull.at[b, g_mine], g2s_sem.at[b, k], g2r_sem.at[b, k], peer
            )
            cc = fold_copy(
                cfull.at[b, c_mine], cfull.at[b, c_mine], c2s_sem.at[b, k], c2r_sem.at[b, k], peer
            )
            gc.start()
            cc.start()
            second[b] += [gc, cc]
            pending += [gc, cc]

    feat_copies = []
    feat_local = []
    for b in range(blocks):
        for copy in small[b]:
            copy.wait_recv()
        cols = jnp.concatenate([stats[b, j, 0:1, :] for j in range(n_f)], axis=0)
        psums = jnp.concatenate([stats[b, j, 2:3, :] for j in range(n_f)], axis=0)
        within = stats[b, 0, 1:2, :]
        for j in range(1, n_f):
            within += stats[b, j, 1:2, :]
        mean = jnp.sum(cols, axis=0, keepdims=True) * (1.0 / total_rows)
        shift = cols * (1.0 / rows) - mean
        between = jnp.sum(shift * shift, axis=0, keepdims=True) * float(rows)
        inv = 1.0 / jnp.sqrt((within + between) * (1.0 / total_rows) + EPSILON)
        inv_down = down(inv)
        others = jnp.where(iota((n_f, B), 0) == me_f, 0.0, shift)
        others_t = jnp.transpose(others)
        psums_t = jnp.transpose(psums)[:traits, :]
        for copy in second[b]:
            copy.wait_recv()
        diag_out = within - stats[b, me_f, 1:2, :]
        eye = iota((T, T), 0) == iota((T, T), 1)
        reach = [jnp.zeros((1, T), F32) for _ in range(B // T)]
        for slot, (i, j) in enumerate(TILES):
            si, sj = slice(i * T, (i + 1) * T), slice(j * T, (j + 1) * T)
            sp = slice(slot * T, (slot + 1) * T)
            outer = dot_nn(others_t[si, :], others[:, sj], HIGH)
            tile = gfull[b, sp, :].astype(F32) - gsend[b, sp, :].astype(F32)
            if i == j:
                tile = jnp.where(eye, diag_out[:, sj], tile)
            tile = tile + float(rows) * outer
            tile = inv_down[si, :] * tile * (inv[:, sj] * (1.0 / held))
            reach[j] += jnp.sum(jnp.abs(tile), axis=0, keepdims=True)
            hi = tile.astype(BF16)
            s_hi[si, sj] = hi
            s_lo[si, sj] = (tile - hi.astype(F32)).astype(BF16)
            if i != j:
                tile = tile.T
                reach[i] += jnp.sum(jnp.abs(tile), axis=0, keepdims=True)
                hi = tile.astype(BF16)
                s_hi[sj, si] = hi
                s_lo[sj, si] = (tile - hi.astype(F32)).astype(BF16)
        bound = jnp.max(jnp.concatenate(reach, axis=1), axis=1, keepdims=True)
        moved = dot_nn(psums_t, others, HIGH)
        target = jnp.concatenate(
            [
                cfull[b, i * traits : (i + 1) * traits, :]
                - csend[b, i * traits : (i + 1) * traits, :]
                for i in range(B // T)
            ],
            axis=1,
        )
        target = (target + moved) * (inv * (1.0 / held))
        line = iota((R * traits, traits), 0)
        spread = iota((R * traits, traits), 1) == (line // group) * own + line % own
        target = dot_nn(spread.astype(F32), target, HIGH)
        low = jnp.where(
            (iota((R * traits, 1), 0) // own) % R == 0, F32(LAMBDAS[0]), F32(LAMBDAS[1])
        )
        high = low + bound
        center = 0.5 * (high + low)
        radius = 0.5 * (high - low)
        sigma = center / radius
        rho = 1.0 / sigma
        direction = target / center
        residual = target
        coef = jnp.zeros_like(target)
        for step in range(ITERS):
            coef = coef + direction
            if step + 1 < ITERS:
                d_hi = direction.astype(BF16)
                d_lo = (direction - d_hi.astype(F32)).astype(BF16)
                both = dot_nn(jnp.concatenate([d_hi, d_lo], axis=0), s_hi[...])
                times = both[: R * traits] + both[R * traits :] + dot_nn(d_hi, s_lo[...])
                residual = residual - (times + low * direction)
                rho_next = 1.0 / (2.0 * sigma - rho)
                direction = rho_next * rho * direction + 2.0 * rho_next / radius * residual
                rho = rho_next
        scaled = (coef * inv).astype(BF16)
        offset = jnp.sum(scaled.astype(F32) * mean, axis=1, keepdims=True)

        @pl.loop(0, chunks)
        def _(c, b=b, scaled=scaled, offset=offset):
            part = pl.ds(pl.multiple_of(c * CHUNK, CHUNK), CHUNK)
            feat = (dot_nt(scaled, xbuf[b, part, :]) - offset).astype(BF16)
            for d in range(n_b):
                fsend[b, d, :, part] = feat[d * group : (d + 1) * group, :]

        slot = me_b * blocks + b
        for k, peer in enumerate(blk_peers):
            copy = pltpu.make_async_remote_copy(
                src_ref=fsend.at[b, peer], dst_ref=frecv.at[slot],
                send_sem=fs_sem.at[b, k], recv_sem=fr_sem.at[b, k],
                device_id=(me_f, peer), device_id_type=MESH,
            )
            copy.start()
            feat_copies.append(copy)
            pending.append(copy)
        keep = pltpu.make_async_copy(fsend.at[b, me_b], frecv.at[slot], fl_sem.at[b])
        keep.start()
        feat_local.append(keep)

    for copy in feat_local:
        copy.wait()
    for copy in feat_copies:
        copy.wait_recv()

    def level(c):
        part = pl.ds(pl.multiple_of(c * CHUNK, CHUNK), CHUNK)
        return frecv[:, :, part].reshape(lanes, CHUNK), part

    def add_level(c, carry):
        hg, hc = carry
        feat, part = level(c)
        return hg + dot_nt(feat, feat), hc + dot_nt(pa[:traits, part], feat)

    hg, hc = lax.fori_loop(
        0, chunks, add_level, (jnp.zeros((lanes, lanes), F32), jnp.zeros((traits, lanes), F32))
    )
    same = iota((lanes, lanes), 0) % own == iota((lanes, lanes), 1) % own
    gather = (iota((q_total, lanes), 1) // own == iota((q_total, lanes), 0)).astype(F32)
    compact = dot_nn(gather, jnp.where(same, hg, 0.0), HIGH)
    mine = iota((traits, lanes), 0) == me_b * own + iota((traits, lanes), 1) % own
    right = jnp.sum(jnp.where(mine, hc, 0.0), axis=0, keepdims=True)
    hbuf[me_f, :q_total, :] = compact
    hbuf[me_f, q_total:, :] = jnp.broadcast_to(right, (8, lanes))
    h_copies = []
    for k, peer in enumerate(fold_peers):
        copy = fold_copy(hbuf.at[me_f], hbuf.at[me_f], hs_sem.at[k], hr_sem.at[k], peer)
        copy.start()
        h_copies.append(copy)
        pending.append(copy)
    for copy in h_copies:
        copy.wait_recv()
    hoo = jnp.zeros((q_total + 8, lanes), F32)
    for j in range(n_f):
        hoo += jnp.where(me_f == j, 0.0, hbuf[j])
    hoo = hoo * (1.0 / held)

    def all_groups(a):
        shift = own
        while shift < lanes:
            a = a + pltpu.roll(a, shift, 1)
            shift *= 2
        return a

    feature_of = iota((q_total, lanes), 1) // own
    on_diag = feature_of == iota((q_total, lanes), 0)
    system = hoo[:q_total]
    trace = jnp.sum(all_groups(jnp.where(on_diag, system, 0.0)), axis=0, keepdims=True)
    system = system + jnp.where(on_diag, (LEVEL_ONE / q_total) * trace, 0.0)
    rhs = all_groups(jnp.where(on_diag, hoo[q_total : q_total + 1], 0.0))
    for q in range(q_total):
        column = all_groups(jnp.where(feature_of == q, system, 0.0))
        inverse = 1.0 / column[q : q + 1]
        pivot = system[q : q + 1] * inverse
        pivot_rhs = rhs[q : q + 1] * inverse
        here = iota((q_total, lanes), 0) == q
        system = jnp.where(here, pivot, system - column * pivot)
        rhs = jnp.where(here, pivot_rhs, rhs - column * pivot_rhs)
    weight = jnp.sum(jnp.where(on_diag, rhs, 0.0), axis=0, keepdims=True)
    pad = 16
    weight = jnp.where(iota((pad, lanes), 1) % own == iota((pad, lanes), 0), weight, 0.0)
    w_hi = weight.astype(BF16)
    rest = weight - w_hi.astype(F32)
    w_mid = rest.astype(BF16)
    w_lo = (rest - w_mid.astype(F32)).astype(BF16)
    w_all = jnp.concatenate([w_hi, w_mid, w_lo], axis=0)

    @pl.loop(0, chunks)
    def _(c):
        feat, part = level(c)
        three = dot_nn(w_all, feat)
        out_ref[:, part] = (three[:pad] + three[pad : 2 * pad] + three[2 * pad :])[:own]

    for copy in pending:
        copy.wait_send()


def per_device(genotypes, phenotypes, trait_order):
    n_f = lax.axis_size("fold")
    n_b = lax.axis_size("blk")
    rows, variants = genotypes.shape
    blocks = variants // B
    traits = phenotypes.shape[0]
    own = traits // n_b
    q_total = n_b * blocks * R
    lanes = q_total * own
    c_all = (B // T) * traits
    dma = pltpu.SemaphoreType.DMA
    vmem = pltpu.VMEM
    return pl.pallas_call(
        functools.partial(kernel, n_f, n_b),
        out_shape=jax.ShapeDtypeStruct((own, rows), F32),
        in_specs=[
            pl.BlockSpec(memory_space=pltpu.VMEM),
            pl.BlockSpec(memory_space=pltpu.VMEM),
            pl.BlockSpec(memory_space=pl.ANY),
        ],
        out_specs=pl.BlockSpec(memory_space=pltpu.VMEM),
        scratch_shapes=[
            vmem((blocks, rows, B), BF16),
            vmem((traits + 16, rows), BF16),
            vmem((B, B), F32),
            vmem((traits + 16, B), F32),
            vmem((blocks, PACK, T), BF16),
            vmem((blocks, n_f, PACK // n_f, T), BF16),
            vmem((blocks, PACK, T), BF16),
            vmem((blocks, c_all, T), F32),
            vmem((blocks, n_f, c_all // n_f, T), F32),
            vmem((blocks, c_all, T), F32),
            vmem((blocks, n_f, 8, B), F32),
            vmem((B, B), BF16),
            vmem((B, B), BF16),
            vmem((blocks, n_b, R * own, rows), BF16),
            vmem((n_b * blocks, R * own, rows), BF16),
            vmem((n_f, q_total + 8, lanes), F32),
            dma((blocks, rows // CHUNK)),
        ]
        + [dma((blocks, n_f - 1)) for _ in range(10)]
        + [dma((blocks, n_b - 1)) for _ in range(2)]
        + [dma((blocks,))]
        + [dma((n_f - 1,)) for _ in range(2)],
        compiler_params=pltpu.CompilerParams(
            collective_id=0, has_side_effects=True, vmem_limit_bytes=52 * 1024 * 1024
        ),
    )(trait_order.reshape(1, traits), phenotypes, genotypes)


def solution(mesh):
    return jax.shard_map(
        per_device,
        mesh=mesh,
        in_specs=(P("fold", "blk"), P(None, "fold"), P()),
        out_specs=P("blk", "fold"),
        check_vma=False,
    )
```

time: 352 us -> 93.3 us (0.27)
  local copies, waits for them, and re-layouts: 105 us -> 2.4 us
  Pallas kernels: 0 us -> 89.2 us
  waiting for transfers between devices: 76.8 us -> 0 us
  matrix products: 64.6 us -> 0 us
  blocking collectives: 59.4 us -> 0 us
  other arithmetic: 27.2 us -> 0 us
  between operations: 13.7 us -> 0.01 us
  starting transfers between devices: 3.61 us -> 0 us
    pallas_call x0 -> x1, Pallas kernels: none -> 89.2 us  [per_device(): pl.pallas_call(functools.partial(kernel, n_f, n_b), out_shape=jax.ShapeDt...]
    dot_general x15 -> x0, matrix products: 64.1 us -> none  [the longest x1 18.2 us: local_gram(): jnp.einsum('sbi,sbj->bij', geno_blocks, geno_blocks, preferred_element_ty...]
    psum x1 -> x0, local copies, waits for them, and re-layouts: 60.1 us -> none  [per_device(): gram_sum, cross_total = lax.psum((gram_part, cross_local), 'fold')]
    psum x2 -> x0, blocking collectives: 59.4 us -> none  [the longest x1 35.9 us: per_device(): hgram_total, hcross_total = lax.psum((hgram_own, hcross_own), 'fold')]
    psum x1 -> x0, waiting for transfers between devices: 51.2 us -> none  [per_device(): gram_sum, cross_total = lax.psum((gram_part, cross_local), 'fold')]
    reshape x2 -> x0, local copies, waits for them, and re-layouts: 30.6 us -> none  [the longest x1 27.9 us: per_device(): geno_blocks = genotypes.reshape(sample_rows, block_count, B)]
    all_to_all x1 -> x0, waiting for transfers between devices: 25.6 us -> none  [per_device(): lax.all_to_all(feature, 'blk', split_axis=0, concat_axis=1, tiled=True)]
    another operation x7 -> x0, other arithmetic: 21.8 us -> none  [the longest x4 11.9 us: per_device(): factor = jnp.linalg.cholesky(level_system)]
  transfers between devices with their start and end apart: 2 -> 0, of which waited for: 2 -> 0; matrix products, arithmetic and copies ran while one was open for 10% -> 0% of each run, Pallas kernels for 0% -> 0%
where the time goes in v1:
time: 93.3 us; the launch traced here: 91.7 us
  Pallas kernels  89.2 us (96%)
  local copies, waits for them, and re-layouts  2.4 us (3%)
    pallas_call x1, Pallas kernels, per_device(): pl.pallas_call(functools.partial(kernel, n_f, n_b), out_shape=jax.ShapeDt...  89.2 us
    unnamed x5, local copies, waits for them, and re-layouts  2.4 us

profile of v1, /device:TPU:0, one launch (start us, length us, event | category | flops | bytes accessed | tf_op | source)
XLA Modules:
  0.0 91.7 jit_solution(13392282642670232815)
XLA Ops:
  0.0 0.0 copy-start
  0.0 1.0 %copy-done = bf16[32,8192]{1,0:T(8,128)(2,1)S(1)} copy-done((bf16[32,8192]{1,0:T(8,128)(2,1)S(1)}, bf16[32,8192]{1,0:T(8,128)(2,1)}, u32[]{:S(2)}) %copy-start) | copy-done | bytes 524312
  1.0 0.0 copy-start.1
  1.0 0.7 copy-done.1
  1.7 89.2 %shard_map.37 = f32[8,8192]{1,0:T(8,128)S(1)} custom-call(s32[1,32]{1,0:T(1,128)S(1)} %bitcast.1, bf16[32,8192]{1,0:T(8,128)(2,1)S(1)} %copy-done, bf16[8192,1024]{1,0:T(8,128)(2,1)} %geno_ref.1), custom_call_target="tpu_custom_call" | custom-call | tf_op jit(solution)/shard_map/pallas_call | solution.py:378
  90.9 0.7 copy.5
Async XLA Ops:
  0.0 1.0 %copy-start = (bf16[32,8192]{1,0:T(8,128)(2,1)S(1)}, bf16[32,8192]{1,0:T(8,128)(2,1)}, u32[]{:S(2)}) copy-start(bf16[32,8192]{1,0:T(8,128)(2,1)} %phen_ref.1) | copy-start | bytes 1572868
  1.0 0.7 copy-start.1
